TPU v7x, 32 devices: a whole 2x2x4 slice. The times are simulated.
32 devices in a mesh: req: 8 (over z, y), mp: 4 (over x, core).
Axes of the slice: x: 2, y: 2, z: 4, core: 2. Of those that a mesh axis runs over, the one named last changes fastest.
Arguments:
- queries: bfloat16 [4, 64, 4096], P(None, 'req', 'mp'), may hold values from -1200 to 1200
- fresh_key_value: bfloat16 [4, 2, 64, 2048], P(None, None, 'req', 'mp'), may hold values from -6 to 6
- suffix_key_value: bfloat16 [2, 64, 128, 2048], P(None, 'req', None, 'mp'), may hold values from -6 to 6
- suffix_len: int32 [64], P('req'), may hold values from 1 to 128
- prefix_ids: int32 [64], P('req'), may hold values from 0 to 3
- panel_owner: int32 [8], P('req'), may hold values from 0 to 7, each once
- prefix_key_value: bfloat16 [2, 8, 2048, 2048], P(None, 'req', None, 'mp'), may hold values from -6 to 6
- out_weight: bfloat16 [4096, 4608], P('mp'), may hold values from -0.09375 to 0.09375
- swap_flags: int32 [4, 64], P(None, 'req'), may hold values from 0 to 1, as said below
Outputs:
- attn_out: bfloat16 [4, 64, 4608], P(None, 'req', 'mp')
Inputs may be any that keep to these rules, and one draw needn't show every extreme that they name: `swap_flags`: in each step exactly 2 slots of every device are flagged, and a device and its partner of that step flag the same slots.
All inputs are finite; a program needn't handle non-finite values.
Results may differ from a plain program's by a relative error of at most 0.0057.
Values may be sent and summed in bfloat16 or wider, within the bound.
A program may use at most 384 MiB of HBM per device.

v0:
```python
import jax
import jax.numpy as jnp
from jax import lax
from jax.sharding import PartitionSpec as P

D = 4608
QUERY_HEADS = 32
HEAD_DIMENSION = 128
SUFFIX_SLOTS = 128
PANEL_TOKENS = 2048
DECODE_STEPS = 4


NEG = -1e30


def partner(value, axis, distance):
    mask = 2**distance
    pairs = [(source, source ^ mask) for source in range(lax.axis_size(axis))]
    return lax.ppermute(value, axis, pairs)


def block_stats(scores, is_valid, values_block, pattern):
    masked = jnp.where(is_valid, scores, NEG)
    peak_value = jnp.max(masked, axis=-1)
    weights = jnp.where(is_valid, jnp.exp(masked - peak_value[..., None]), 0.0).astype(jnp.bfloat16)
    total = jnp.sum(weights.astype(jnp.float32), axis=-1)
    summed = jnp.einsum(pattern, weights, values_block, preferred_element_type=jnp.float32)
    return (peak_value, total, summed)


def shards(
    queries,
    fresh_key_value,
    suffix_key_value,
    suffix_len,
    prefix_ids,
    panel_owner,
    prefix_key_value,
    out_weight,
    swap_flags,
):
    row_count = suffix_key_value.shape[1]
    kv_local = suffix_key_value.shape[3] // HEAD_DIMENSION
    heads_local = queries.shape[2] // HEAD_DIMENSION
    query_group_count = heads_local // kv_local
    score_scale = (D // QUERY_HEADS) ** (-0.5)
    bit_count = lax.axis_size("req").bit_length() - 1
    row_start = lax.axis_index("req") * row_count
    request_suffix_cache = suffix_key_value
    past_tokens = jnp.zeros((2, row_count, DECODE_STEPS, kv_local * HEAD_DIMENSION), jnp.bfloat16)
    lengths = suffix_len
    prefix_of = prefix_ids
    my_prefix = panel_owner[0] // 2
    shared_panel_keys = prefix_key_value[0, 0].reshape(PANEL_TOKENS, kv_local, HEAD_DIMENSION)
    shared_panel_values = prefix_key_value[1, 0].reshape(PANEL_TOKENS, kv_local, HEAD_DIMENSION)
    position = jnp.arange(SUFFIX_SLOTS + DECODE_STEPS, dtype=jnp.int32)
    results = []
    for decode_step_index in range(DECODE_STEPS):
        pair_bit = decode_step_index % bit_count
        is_moved = swap_flags[decode_step_index] == 1
        far_cache, far_history = partner((request_suffix_cache, past_tokens), "req", pair_bit)
        far_lengths, far_prefix = partner((lengths, prefix_of), "req", pair_bit)
        request_suffix_cache = jnp.where(
            is_moved[None, :, None, None], far_cache, request_suffix_cache
        )
        past_tokens = jnp.where(is_moved[None, :, None, None], far_history, past_tokens)
        lengths = jnp.where(is_moved, far_lengths, lengths)
        prefix_of = jnp.where(is_moved, far_prefix, prefix_of)
        past_tokens = past_tokens.at[:, :, decode_step_index].set(
            fresh_key_value[decode_step_index]
        )
        query_matrix = queries[decode_step_index]
        query_block = query_matrix.reshape(row_count, kv_local, query_group_count, HEAD_DIMENSION)
        request_keys = jnp.concatenate([request_suffix_cache[0], past_tokens[0]], axis=1).reshape(
            row_count, SUFFIX_SLOTS + DECODE_STEPS, kv_local, HEAD_DIMENSION
        )
        request_values = jnp.concatenate([request_suffix_cache[1], past_tokens[1]], axis=1).reshape(
            row_count, SUFFIX_SLOTS + DECODE_STEPS, kv_local, HEAD_DIMENSION
        )
        own_scores = (
            jnp.einsum(
                "rkgd,rtkd->rkgt", query_block, request_keys, preferred_element_type=jnp.float32
            )
            * score_scale
        )
        is_valid = jnp.where(
            position[None, :] < SUFFIX_SLOTS,
            position[None, :] < lengths[:, None],
            position[None, :] - SUFFIX_SLOTS <= decode_step_index,
        )
        request_maximum, request_denominator_sum, request_weighted_sum = block_stats(
            own_scores, is_valid[:, None, None, :], request_values, "rkgt,rtkd->rkgd"
        )
        all_queries = lax.all_gather(query_matrix, "req", axis=0, tiled=True)
        all_prefix = lax.all_gather(prefix_of, "req", axis=0, tiled=True)
        matched = all_prefix == my_prefix
        all_block = all_queries.reshape(
            all_queries.shape[0], kv_local, query_group_count, HEAD_DIMENSION
        )
        panel_scores = (
            jnp.einsum(
                "rkgd,tkd->rkgt", all_block, shared_panel_keys, preferred_element_type=jnp.float32
            )
            * score_scale
        )
        panel_peak, panel_total, panel_sum = block_stats(
            panel_scores, matched[:, None, None, None], shared_panel_values, "rkgt,tkd->rkgd"
        )
        global_peak = lax.pmax(panel_peak, "req")
        factor = jnp.exp(panel_peak - global_peak)
        prefix_sum, prefix_total = (
            lax.psum_scatter(panel_sum * factor[..., None], "req", scatter_dimension=0, tiled=True),
            lax.psum_scatter(panel_total * factor, "req", scatter_dimension=0, tiled=True),
        )
        prefix_peak = lax.dynamic_slice_in_dim(global_peak, row_start, row_count, 0)
        overall = jnp.maximum(request_maximum, prefix_peak)
        own_factor = jnp.exp(request_maximum - overall)
        prefix_factor = jnp.exp(prefix_peak - overall)
        numerator = (
            request_weighted_sum * own_factor[..., None] + prefix_sum * prefix_factor[..., None]
        )
        denominator = request_denominator_sum * own_factor + prefix_total * prefix_factor
        attended = (
            (numerator / denominator[..., None])
            .reshape(row_count, heads_local * HEAD_DIMENSION)
            .astype(jnp.bfloat16)
        )
        results.append(attended)
    stacked = jnp.stack(results).reshape(DECODE_STEPS * row_count, heads_local * HEAD_DIMENSION)
    partial_sums = jnp.dot(stacked, out_weight, preferred_element_type=jnp.float32)
    summed = lax.psum_scatter(partial_sums, "mp", scatter_dimension=1, tiled=True)
    return summed.reshape(DECODE_STEPS, row_count, summed.shape[1]).astype(jnp.bfloat16)


def solution(mesh):
    placed = (
        P(None, "req", "mp"),
        P(None, None, "req", "mp"),
        P(None, "req", None, "mp"),
        P("req"),
        P("req"),
        P("req"),
        P(None, "req", None, "mp"),
        P("mp", None),
        P(None, "req"),
    )
    return jax.shard_map(
        shards, mesh=mesh, in_specs=placed, out_specs=P(None, "req", "mp"), check_vma=False
    )
```

profile of v0, /device:TPU:0, one launch (start us, length us, event | category | flops | bytes accessed | tf_op | source)
XLA Modules:
  0.0 566.6 jit_solution(11399890668646246947)
XLA Ops:
  6.5 3.0 collective-permute-start
  9.6 2.1 collective-permute-start.2
  11.6 4.0 copy.198
  17.0 69.8 %all-gather.2 = bf16[1,64,1024]{2,1,0:T(8,128)(2,1)S(1)} all-gather(bf16[1,8,1024]{2,1,0:T(8,128)(2,1)S(1)} %get-tuple-element.130), channel_id=4, replica_groups=mesh['req'=8,'mp'=4] {'req'}, dimensions={1}, use_global_device_ids=true | all-gather | bytes 147456 | tf_op jit(solution)/shard_map/all_gather | solution.py:95
  87.4 30.5 %all-gather.3 = bf16[1,64,1024]{2,1,0:T(8,128)(2,1)S(1)} all-gather(bf16[1,8,1024]{2,1,0:T(8,128)(2,1)S(1)} %get-tuple-element.129), channel_id=5, replica_groups=mesh['req'=8,'mp'=4] {'req'}, dimensions={1}, use_global_device_ids=true | all-gather | bytes 147456 | tf_op jit(solution)/shard_map/all_gather | solution.py:95
  118.0 30.5 %all-gather.1 = bf16[1,64,1024]{2,1,0:T(8,128)(2,1)S(1)} all-gather(bf16[1,8,1024]{2,1,0:T(8,128)(2,1)S(1)} %get-tuple-element.128), channel_id=3, replica_groups=mesh['req'=8,'mp'=4] {'req'}, dimensions={1}, use_global_device_ids=true | all-gather | bytes 147456 | tf_op jit(solution)/shard_map/all_gather | solution.py:95
  148.5 30.5 %all-gather = bf16[1,64,1024]{2,1,0:T(8,128)(2,1)S(1)} all-gather(bf16[1,8,1024]{2,1,0:T(8,128)(2,1)S(1)} %get-tuple-element.127), channel_id=2, replica_groups=mesh['req'=8,'mp'=4] {'req'}, dimensions={1}, use_global_device_ids=true | all-gather | bytes 147456 | tf_op jit(solution)/shard_map/all_gather | solution.py:95
  179.4 4.5 fusion.173
  183.9 2.9 copy.315
  186.9 4.0 copy.314
  192.9 2.0 collective-permute-start.4
  194.9 1.5 collective-permute-done.7
  197.7 2.0 collective-permute-start.8
  199.6 1.5 collective-permute-done.11
  202.2 3.0 collective-permute-start.15
  206.7 2.0 collective-permute-done.12
  208.8 8.6 %all-reduce.12 = (s32[64]{0:T(128)S(1)}, s32[64]{0:T(128)S(1)}, s32[64]{0:T(128)S(1)}, s32[64]{0:T(128)S(1)}) all-reduce(s32[64]{0:T(128)S(1)} %get-tuple-element.133, s32[64]{0:T(128)S(1)} %get-tuple-element.109, s32[64]{0:T(128)S(1)} %get-tuple-element.107, s32[64]{0:T(128)S(1)} %get-tuple-element.105), channel_id=1, replica_groups=mesh['req'=8,'mp'=4] {'req'}, use_global_device_ids=true, to_apply=%add.3 | all-reduce | flops 256 | bytes 2048
  217.5 4.5 bitcast_reduce_fusion
  222.0 2.9 bitcast_reduce_fusion.1
  225.8 2.4 convert_reduce_fusion.2
  229.2 2.4 convert_reduce_fusion.3
  231.6 35.8 %all-reduce.15 = (f32[64,4,2]{0,1,2:T(4,128)S(1)}, f32[64,4,2]{0,1,2:T(4,128)S(1)}, f32[64,4,2]{0,1,2:T(4,128)S(1)}, f32[64,4,2]{0,1,2:T(4,128)S(1)}) all-reduce(f32[64,4,2]{0,1,2:T(4,128)S(1)} %copy.275, f32[64,4,2]{0,1,2:T(4,128)S(1)} %copy.253, f32[64,4,2]{0,1,2:T(4,128)S(1)} %copy.231, ...), channel_id=1, replica_groups=mesh['req'=8,'mp'=4] {'req'}, use_global_device_ids=true, to_apply=%region_23.24 | all-reduce | flops 2048 | bytes 16384 | tf_op jit(solution)/shard_map/pmax | solution.py:110
  267.4 2.4 fusion.14
  280.2 37.8 %all-reduce.13 = (f32[64,4,2]{1,2,0:T(2,128)S(1)}, f32[64,4,2]{1,2,0:T(2,128)S(1)}, f32[64,4,2]{1,2,0:T(2,128)S(1)}, f32[64,4,2]{1,2,0:T(2,128)S(1)}) all-reduce(f32[64,4,2]{1,2,0:T(2,128)S(1)} %copy.287, f32[64,4,2]{1,2,0:T(2,128)S(1)} %copy.265, f32[64,4,2]{1,2,0:T(2,128)S(1)} %copy.243, ...), channel_id=13, replica_groups=mesh['req'=8,'mp'=4] {'req'}, use_global_device_ids=true, to_apply=%region_27.28.clone | all-reduce | flops 2048 | bytes 16384
  318.7 2.5 broadcast_select_fusion.3
  323.8 2.1 collective-permute-start.6
  326.0 57.2 %collective-permute-done.6 = bf16[2,8,4,512]{3,1,2,0:T(8,128)(2,1)S(1)} collective-permute-done((bf16[2,8,4,512]{3,1,2,0:T(8,128)(2,1)S(1)}, bf16[2,8,4,512]{3,1,2,0:T(8,128)(2,1)S(1)}, u32[]{:S(2)}, u32[]{:S(2)}) %collective-permute-start.6) | collective-permute-done | bytes 65568 | tf_op jit(solution)/shard_map/ppermute | solution.py:20
  383.3 8.9 %collective-permute-start.10 = (bf16[2,8,4,512]{3,1,2,0:T(8,128)(2,1)S(1)}, bf16[2,8,4,512]{3,1,2,0:T(8,128)(2,1)S(1)}, u32[]{:S(2)}, u32[]{:S(2)}) collective-permute-start(bf16[2,8,4,512]{3,1,2,0:T(8,128)(2,1)S(1)} %bitcast_dynamic-update-slice_fusion.2), channel_id=1, source_target_pairs={{0,16},{4,20},{8,24},{12,28},{16,0},{20,4},{24,8},{28,12},{1,17},{... | collective-permute-start | bytes 196616 | tf_op jit(solution)/shard_map/ppermute | solution.py:20
  392.9 1.5 collective-permute-done.10
  394.5 3.2 broadcast_select_fusion.2
  397.7 2.9 collective-permute-start.9
  400.6 2.7 collective-permute-start.14
  404.0 1.5 collective-permute-done.14
  406.4 48.2 %all-reduce.18.cloned.1.call-done = (f32[64,4,2,128]{3,1,2,0:T(4,128)}, f32[64,4,2,128]{3,1,2,0:T(4,128)}, f32[64,4,2,128]{3,1,2,0:T(4,128)}, f32[64,4,2,128]{3,1,2,0:T(4,128)}) async-done(((f32[64,4,2,128]{3,1,2,0:T(4,128)}, f32[64,4,2,128]{3,1,2,0:T(4,128)}, f32[64,4,2,128]{3,1,2,0:T(4,128)}, f32[64,4,2,128]{3,1,2,0:T(4,128)}), (f32[64,4,2,128]{3,1,2,0:T(4,128)}, f32[64,4,2,128]{3,1,2,0:T(4,128)}, ...) | async-done | bytes 1048592
  460.6 2.3 copy.203
  465.0 2.5 broadcast_select_fusion.1
  469.0 2.7 fusion.175
  471.7 2.3 copy.227
  475.3 2.0 bitcast_reduce_fusion.6
  480.5 1.7 fusion.83
  484.7 2.3 copy.249
  488.3 2.0 bitcast_reduce_fusion.5
  490.4 24.8 %collective-permute-done.13 = bf16[2,8,128,512]{2,3,1,0:T(8,128)(2,1)} collective-permute-done((bf16[2,8,128,512]{2,3,1,0:T(8,128)(2,1)S(1)}, bf16[2,8,128,512]{2,3,1,0:T(8,128)(2,1)}, u32[]{:S(2)}, u32[]{:S(2)}) %collective-permute-start.13) | collective-permute-done | bytes 2097184 | tf_op jit(solution)/shard_map/ppermute | solution.py:20
  515.3 1.9 broadcast_select_fusion
  519.4 2.0 bitcast_reduce_fusion.4
  523.8 6.2 %fusion.100 = f32[32,4608]{1,0:T(8,128)} fusion(bf16[1024,4608]{1,0:T(8,128)(2,1)} %param.24, bf16[1,8,1024]{2,1,0:T(8,128)(2,1)S(1)} %convert_element_type.129, bf16[1,8,1024]{2,1,0:T(8,128)(2,1)S(1)} %convert_element_type.123, bf16[1,8,1024]{2,1,0:T(8,128)(2,1)S(1)} %convert_element_type.117, bf16[1,8,1024]{2,1,0:T(8,128)(2,1)S(1)} %convert_element_type.111), kind=kOutput, calls=%fused_computation.98 | convolution fusion | flops 302088192 | bytes 10092544 | tf_op jit(solution)/shard_map/dot_general | solution.py:131
  530.0 28.1 %reduce-scatter.2.cloned.1.call-done = f32[32,1152]{1,0:T(8,128)} async-done(((f32[32,4608]{1,0:T(8,128)}), f32[32,1152]{1,0:T(8,128)}) %reduce-scatter.2.cloned.1.call-update) | async-done | bytes 147472 | tf_op jit(solution)/shard_map/reduce_scatter | solution.py:132
  558.2 1.6 convert_bitcast_fusion
  (211 shorter events, 46.8 us)
Async XLA Ops:
  6.5 448.0 %all-reduce.18.cloned.1.call-start = ((), (), s32[]{:S(2)}) async-start(), calls=%async_computation.2 | async-start | bytes 2097152
  6.5 186.2 %collective-permute-start = (s32[8]{0:T(128)}, s32[8]{0:T(128)S(1)}, u32[]{:S(2)}, u32[]{:S(2)}) collective-permute-start(s32[8]{0:T(128)} %param.20), channel_id=1, source_target_pairs={{0,4},{4,0},{8,12},{12,8},{16,20},{20,16},{24,28},{28,24},{1,5},{5... | collective-permute-start | bytes 104 | tf_op jit(solution)/shard_map/ppermute | solution.py:20
  9.5 183.3 %collective-permute-start.3 = (s32[8]{0:T(128)}, s32[8]{0:T(128)S(1)}, u32[]{:S(2)}, u32[]{:S(2)}) collective-permute-start(s32[8]{0:T(128)} %param.21), channel_id=1, source_target_pairs={{0,4},{4,0},{8,12},{12,8},{16,20},{20,16},{24,28},{28,24},{1,5},{5... | collective-permute-start | bytes 104 | tf_op jit(solution)/shard_map/ppermute | solution.py:20
  9.5 6.8 %copy-start.6 = (bf16[4,8,1024]{2,1,0:T(8,128)(2,1)S(1)}, bf16[4,8,1024]{2,1,0:T(8,128)(2,1)}, u32[]{:S(2)}) copy-start(bf16[4,8,1024]{2,1,0:T(8,128)(2,1)} %param.17) | copy-start | bytes 196612
  9.6 169.5 %copy-start.21 = (s32[4,8]{1,0:T(4,128)S(1)}, s32[4,8]{1,0:T(4,128)}, u32[]{:S(2)}) copy-start(s32[4,8]{1,0:T(4,128)} %param.25) | copy-start | bytes 388
  9.6 314.2 %collective-permute-start.2 = (bf16[2,8,4,512]{3,1,2,0:T(8,128)(2,1)S(1)}, bf16[2,8,4,512]{3,1,2,0:T(8,128)(2,1)S(1)}, u32[]{:S(2)}, u32[]{:S(2)}) collective-permute-start(bf16[2,8,4,512]{3,1,2,0:T(8,128)(2,1)S(1)} %broadcast_in_dim.269), channel_id=1, source_target_pairs={{0,4},{4,0},{8,12},{12,8},{16,20},{20,16},{24,28},{28,24},{1,5},{5... | collective-permute-start | bytes 196616 | tf_op jit(solution)/shard_map/ppermute | solution.py:20
  15.6 303.1 %collective-permute-start.1 = (bf16[2,8,128,512]{2,3,1,0:T(8,128)(2,1)}, bf16[2,8,128,512]{2,3,1,0:T(8,128)(2,1)}, u32[]{:S(2)}, u32[]{:S(2)}) collective-permute-start(bf16[2,8,128,512]{2,3,1,0:T(8,128)(2,1)} %copy.198), channel_id=1, source_target_pairs={{0,4},{4,0},{8,12},{12,8},{16,20},{20,16},{24,28},{28,24},{1,5},{5... | collective-permute-start | bytes 6291464 | tf_op jit(solution)/shard_map/ppermute | solution.py:20
  179.0 226.5 %copy-start.22 = (pred[8]{0:T(512)(128)(4,1)}, pred[8]{0:T(512)(128)(4,1)S(1)}, u32[]{:S(2)}) copy-start(pred[8]{0:T(512)(128)(4,1)S(1)} %get-tuple-element.138) | copy-start | bytes 28
  186.8 4.0 copy-start.24
  186.8 5.9 %copy-start.25 = (s32[8]{0:T(128)S(1)}, s32[8]{0:T(128)}, u32[]{:S(2)}) copy-start(s32[8]{0:T(128)} %param.21) | copy-start | bytes 100
  186.9 5.9 %copy-start.26 = (s32[8]{0:T(128)S(1)}, s32[8]{0:T(128)}, u32[]{:S(2)}) copy-start(s32[8]{0:T(128)} %param.20) | copy-start | bytes 100
  192.9 3.5 collective-permute-start.7
  192.9 3.7 collective-permute-start.4
  196.7 4.4 collective-permute-start.11
  197.7 4.4 collective-permute-start.8
  202.2 4.5 collective-permute-start.15
  205.2 3.5 collective-permute-start.12
  217.5 4.5 copy-start
  267.4 2.5 copy-start.16
  267.4 2.5 copy-start.17
  267.4 9.1 %copy-start.11 = (f32[64,4,2]{0,1,2:T(4,128)}, f32[64,4,2]{0,1,2:T(4,128)S(1)}, u32[]{:S(2)}) copy-start(f32[64,4,2]{0,1,2:T(4,128)S(1)} %get-tuple-element.65) | copy-start | bytes 6148
  267.4 9.1 %copy-start.13 = (f32[64,4,2]{0,1,2:T(4,128)}, f32[64,4,2]{0,1,2:T(4,128)S(1)}, u32[]{:S(2)}) copy-start(f32[64,4,2]{0,1,2:T(4,128)S(1)} %get-tuple-element.66) | copy-start | bytes 6148
  267.4 3.4 copy-start.3
  270.8 2.3 copy-start.2
  273.1 2.2 copy-start.1
  318.7 5.1 copy-start.7
  321.2 73.3 %collective-permute-start.5 = (bf16[2,8,128,512]{2,3,1,0:T(8,128)(2,1)S(1)}, bf16[2,8,128,512]{2,3,1,0:T(8,128)(2,1)}, u32[]{:S(2)}, u32[]{:S(2)}) collective-permute-start(bf16[2,8,128,512]{2,3,1,0:T(8,128)(2,1)S(1)} %broadcast_select_fusion.3), channel_id=1, source_target_pairs={{0,8},{4,12},{8,0},{12,4},{16,24},{20,28},{24,16},{28,20},{1,9},{5... | collective-permute-start | bytes 6291464 | tf_op jit(solution)/shard_map/ppermute | solution.py:20
  322.7 235.5 %reduce-scatter.2.cloned.1.call-start = ((), (), s32[]{:S(2)}) async-start(), calls=%async_computation.1 | async-start | bytes 737280 | tf_op jit(solution)/shard_map/reduce_scatter | solution.py:132
  323.8 59.4 %collective-permute-start.6 = (bf16[2,8,4,512]{3,1,2,0:T(8,128)(2,1)S(1)}, bf16[2,8,4,512]{3,1,2,0:T(8,128)(2,1)S(1)}, u32[]{:S(2)}, u32[]{:S(2)}) collective-permute-start(bf16[2,8,4,512]{3,1,2,0:T(8,128)(2,1)S(1)} %bitcast_dynamic-update-slice_fusion.3), channel_id=1, source_target_pairs={{0,8},{4,12},{8,0},{12,4},{16,24},{20,28},{24,16},{28,20},{1,9},{5... | collective-permute-start | bytes 196616 | tf_op jit(solution)/shard_map/ppermute | solution.py:20
  383.3 11.1 %collective-permute-start.10 = (bf16[2,8,4,512]{3,1,2,0:T(8,128)(2,1)S(1)}, bf16[2,8,4,512]{3,1,2,0:T(8,128)(2,1)S(1)}, u32[]{:S(2)}, u32[]{:S(2)}) collective-permute-start(bf16[2,8,4,512]{3,1,2,0:T(8,128)(2,1)S(1)} %bitcast_dynamic-update-slice_fusion.2), channel_id=1, source_target_pairs={{0,16},{4,20},{8,24},{12,28},{16,0},{20,4},{24,8},{28,12},{1,17},{... | collective-permute-start | bytes 196616 | tf_op jit(solution)/shard_map/ppermute | solution.py:20
  397.7 67.3 %collective-permute-start.9 = (bf16[2,8,128,512]{2,3,1,0:T(8,128)(2,1)}, bf16[2,8,128,512]{2,3,1,0:T(8,128)(2,1)}, u32[]{:S(2)}, u32[]{:S(2)}) collective-permute-start(bf16[2,8,128,512]{2,3,1,0:T(8,128)(2,1)} %broadcast_select_fusion.2), channel_id=1, source_target_pairs={{0,16},{4,20},{8,24},{12,28},{16,0},{20,4},{24,8},{28,12},{1,17},{... | collective-permute-start | bytes 6291464 | tf_op jit(solution)/shard_map/ppermute | solution.py:20
  400.6 5.0 collective-permute-start.14
  467.5 47.8 %collective-permute-start.13 = (bf16[2,8,128,512]{2,3,1,0:T(8,128)(2,1)S(1)}, bf16[2,8,128,512]{2,3,1,0:T(8,128)(2,1)}, u32[]{:S(2)}, u32[]{:S(2)}) collective-permute-start(bf16[2,8,128,512]{2,3,1,0:T(8,128)(2,1)S(1)} %broadcast_select_fusion.1), channel_id=1, source_target_pairs={{0,4},{4,0},{8,12},{12,8},{16,20},{20,16},{24,28},{28,24},{1,5},{5... | collective-permute-start | bytes 6291464 | tf_op jit(solution)/shard_map/ppermute | solution.py:20
  477.3 5.2 copy-start.4
  484.7 3.6 copy-start.10
  484.7 3.6 copy-start.20
  487.0 28.2 %copy-start.23 = (pred[8]{0:T(512)(128)(4,1)S(1)}, pred[8]{0:T(512)(128)(4,1)}, u32[]{:S(2)}) copy-start(pred[8]{0:T(512)(128)(4,1)} %copy-done.22) | copy-start | bytes 28
  517.3 2.1 copy-start.9
  517.3 2.1 copy-start.19
  518.0 4.1 copy-start.14
  518.0 4.1 copy-start.18
  518.0 4.2 copy-start.12
  518.0 4.2 copy-start.15
  518.0 4.6 copy-start.5
  518.0 4.6 copy-start.8
Sparse Core Ops, SparseCore 0:
  322.8 131.6 all-reduce.17
  530.2 27.9 reduce-scatter.1
where the time goes:
time: 568 us; the launch traced here: 567 us
  blocking collectives  244 us (43%)
  waiting for transfers between devices  169 us (30%)
  local copies, waits for them, and re-layouts  53.7 us (9%)
  starting transfers between devices  31.6 us (6%)
  matrix products  30.5 us (5%)
  other arithmetic  22.2 us (4%)
  between operations  16 us (3%)
    all_gather x4, blocking collectives, shards(): all_queries = lax.all_gather(query_matrix, 'req', axis=0, tiled=True)  161 us
    ppermute x16, waiting for transfers between devices, partner(): return lax.ppermute(value, axis, pairs)  92.7 us
    unnamed x3, waiting for transfers between devices  48.2 us
    unnamed x2, blocking collectives  46.4 us
    pmax x1, blocking collectives, shards(): global_peak = lax.pmax(panel_peak, 'req')  35.8 us
    ppermute x16, starting transfers between devices, partner(): return lax.ppermute(value, axis, pairs)  31.3 us
    reduce_scatter x1, waiting for transfers between devices, shards(): lax.psum_scatter(partial_sums, 'mp', scatter_dimension=1, tiled=True)  28.1 us
    unnamed x70, local copies, waits for them, and re-layouts  18.2 us
  transfers between devices with their start and end apart: 18, of which 12 were waited for; matrix products, arithmetic and copies ran while one was open for 15% of the time, Pallas kernels for 0%

commit v1 on v0

v1 whole, which is shorter than its diff:
```python
import functools
import math

import jax
import jax.numpy as jnp
from jax import lax
from jax.experimental import pallas as pl
from jax.experimental.pallas import tpu as pltpu
from jax.sharding import PartitionSpec as P

D = 4608
QUERY_HEADS = 32
HEAD_DIMENSION = 128
SUFFIX_SLOTS = 128
PANEL_TOKENS = 2048
DECODE_STEPS = 4
BLOCK_RANKS = 4

NEG = -1e30
EXP2_SCALE = (D // QUERY_HEADS) ** (-0.5) * math.log2(math.e)
MESH = pl.DeviceIdType.MESH
F32 = jnp.float32
BF16 = jnp.bfloat16


def dot_t(left, right):
    return lax.dot_general(left, right, (((1,), (1,)), ((), ())), preferred_element_type=F32)


def iota(shape, dimension):
    return lax.broadcasted_iota(jnp.int32, shape, dimension)


def block_stats(queries, keys, values, is_valid):
    scores = dot_t(queries, keys)
    if is_valid is not None:
        scores = jnp.where(is_valid, scores, NEG)
    peak = jnp.max(scores, axis=1, keepdims=True)
    weights = jnp.exp2((scores - peak) * EXP2_SCALE)
    if is_valid is not None:
        weights = jnp.where(is_valid, weights, 0.0)
    widened = jnp.concatenate([values, jnp.ones(values.shape, BF16)], axis=1)
    summed = jnp.dot(weights.astype(BF16), widened, preferred_element_type=F32)
    return peak, summed[:, :HEAD_DIMENSION], summed[:, HEAD_DIMENSION:]


def kernel(
    n_req,
    n_mp,
    q_hbm,
    fresh_hbm,
    suffix_hbm,
    mask_hbm,
    info_hbm,
    panel_hbm,
    weight_hbm,
    out_ref,
    q_all,
    info_all,
    panel,
    suffix,
    fresh,
    mask,
    weight,
    num_out,
    stat_out,
    num_in,
    stat_in,
    attended,
    part_out,
    part_in,
    local_sem,
    q_send,
    q_recv,
    info_send,
    info_recv,
    num_send,
    num_recv,
    stat_send,
    stat_recv,
    part_send,
    part_recv,
):
    me = lax.axis_index("req")
    mp = lax.axis_index("mp")
    half = n_req // 2
    side = me // half
    place = me % half
    near_base = side * half
    far_base = (1 - side) * half
    kv_local = panel.shape[2] // HEAD_DIMENSION
    rows_rank = q_all.shape[1]
    slots = rows_rank // DECODE_STEPS
    rows = BLOCK_RANKS * rows_rank
    lanes = info_all.shape[2]

    local = [
        pltpu.make_async_copy(q_hbm, q_all.at[me], local_sem.at[0]),
        pltpu.make_async_copy(info_hbm, info_all.at[me], local_sem.at[1]),
        pltpu.make_async_copy(panel_hbm, panel, local_sem.at[2]),
        pltpu.make_async_copy(fresh_hbm, fresh, local_sem.at[3]),
        pltpu.make_async_copy(suffix_hbm, suffix, local_sem.at[4]),
        pltpu.make_async_copy(mask_hbm, mask, local_sem.at[5]),
        pltpu.make_async_copy(weight_hbm, weight, local_sem.at[6]),
    ]
    for copy in local:
        copy.start()

    near = [
        (d, near_base + (place + d) % half, near_base + (place + half - d) % half)
        for d in range(1, half)
    ]
    far = [
        (half + d, far_base + (place + d) % half, far_base + (place + half - d) % half)
        for d in range(half)
    ]
    mp_peers = [(d, (mp + d) % n_mp, (mp + n_mp - d) % n_mp) for d in range(1, n_mp)]
    mp_peers = sorted(mp_peers, key=lambda peer: abs(peer[0] - n_mp // 2))

    barrier = pltpu.get_barrier_semaphore()
    for _, target, _ in near + far:
        pl.semaphore_signal(barrier, inc=1, device_id=(target, mp), device_id_type=MESH)
    for _, target, _ in mp_peers:
        pl.semaphore_signal(barrier, inc=1, device_id=(me, target), device_id_type=MESH)
    pl.semaphore_wait(barrier, n_req - 1 + n_mp - 1)

    def remote(source, destination, send, receive, index, device):
        return pltpu.make_async_remote_copy(
            src_ref=source,
            dst_ref=destination,
            send_sem=send.at[index],
            recv_sem=receive.at[index],
            device_id=device,
            device_id_type=MESH,
        )

    def query_copy(index, target, slot):
        return remote(q_hbm, q_all.at[slot], q_send, q_recv, index, (target, mp))

    def info_copy(index, target, slot):
        return remote(info_hbm, info_all.at[slot], info_send, info_recv, index, (target, mp))

    def num_copy(index, target, slot):
        return remote(
            num_out.at[target], num_in.at[slot], num_send, num_recv, index, (target, mp)
        )

    def stat_copy(index, target, slot):
        return remote(
            stat_out.at[target], stat_in.at[slot], stat_send, stat_recv, index, (target, mp)
        )

    def part_copy(index, target, slot):
        return remote(
            part_out.at[target], part_in.at[slot], part_send, part_recv, index, (me, target)
        )

    for index, target, _ in near + far:
        info_copy(index, target, me).start()
    for index, target, _ in near + far:
        query_copy(index, target, me).start()

    local[1].wait()
    local[5].wait()
    for index, target, source in near + far:
        info_copy(index, target, source).wait_recv()
    info = info_all[0]
    for rank in range(1, n_req):
        info = info + info_all[rank]
    state_row = iota((8, lanes), 0)
    position = iota((8, lanes), 1)
    state = jnp.where(
        state_row == 0,
        position.astype(F32),
        jnp.where(state_row == 1, jnp.broadcast_to(info[4:5], (8, lanes)), 0.0),
    )
    bit_count = n_req.bit_length() - 1
    requests = jnp.zeros((8, lanes), F32)
    for step in range(DECODE_STEPS):
        distance = slots << (step % bit_count)
        lane = iota((lanes, lanes), 1)
        partner = jnp.where((lane // distance) % 2 == 1, lane - distance, lane + distance)
        flag = jnp.broadcast_to(info[step : step + 1], (lanes, lanes)) > 0.5
        origin = jnp.where(flag, partner, lane)
        moves = jnp.where(iota((lanes, lanes), 0) == origin, 1.0, 0.0).astype(BF16)
        state = jnp.dot(state.astype(BF16), moves, preferred_element_type=F32)
        requests = jnp.where(state_row == step, state[0:1], requests)
        requests = jnp.where(state_row == DECODE_STEPS + step, state[1:2], requests)
    requests = requests.astype(BF16)
    token = iota((rows_rank, lanes), 0)
    token_at = jnp.where(iota((rows_rank, lanes), 1) == me * slots + token % slots, 1.0, 0.0)
    token_steps = dot_t(requests, token_at.astype(BF16))
    token_step = iota((1, rows_rank), 1) // slots
    token_request = jnp.zeros((1, rows_rank), F32)
    for step in range(DECODE_STEPS):
        token_request = jnp.where(token_step == step, token_steps[step : step + 1], token_request)
    my_prefix = mask[slots : slots + 1, 0:1]

    def work(first):
        row = iota((rows, lanes), 0)
        row_position = (first + row // rows_rank) * slots + row % slots
        row_at = jnp.where(iota((rows, lanes), 1) == row_position, 1.0, 0.0).astype(BF16)
        down = dot_t(row_at, requests)
        across = dot_t(requests, row_at)
        down_step = (iota((rows, 1), 0) // slots) % DECODE_STEPS
        across_step = (iota((1, rows), 1) // slots) % DECODE_STEPS
        down_request = jnp.zeros((rows, 1), F32)
        down_prefix = jnp.zeros((rows, 1), F32)
        across_request = jnp.zeros((1, rows), F32)
        for step in range(DECODE_STEPS):
            here = down_step == step
            down_request = jnp.where(here, down[:, step : step + 1], down_request)
            down_prefix = jnp.where(
                here, down[:, DECODE_STEPS + step : DECODE_STEPS + step + 1], down_prefix
            )
            across_request = jnp.where(across_step == step, across[step : step + 1], across_request)
        matched = jnp.where(down_prefix == my_prefix, 1.0, 0.0)
        matched = jnp.concatenate([matched, matched], axis=0) > 0.5
        own = iota((rows_rank, rows), 0)
        pick = jnp.where(
            (across_request == (me * slots + own % slots).astype(F32))
            & (across_step == own // slots),
            1.0,
            0.0,
        ).astype(BF16)
        own = iota((rows, rows_rank), 1)
        put = jnp.where(
            (down_request == (me * slots + own % slots).astype(F32)) & (down_step == own // slots),
            1.0,
            0.0,
        )
        is_here = jnp.sum(put, axis=1, keepdims=True)
        is_here = jnp.concatenate([is_here, is_here], axis=0) > 0.5
        fresh_valid = jnp.where(
            (down_request == token_request) & (down_step >= token_step), 1.0, 0.0
        )
        fresh_valid = jnp.concatenate([fresh_valid, fresh_valid], axis=0) > 0.5

        def head(h, carry):
            at = pl.ds(pl.multiple_of(h * HEAD_DIMENSION, HEAD_DIMENSION), HEAD_DIMENSION)
            pair = [
                pl.ds(
                    pl.multiple_of((2 * h + g) * HEAD_DIMENSION, HEAD_DIMENSION), HEAD_DIMENSION
                )
                for g in range(2)
            ]
            query = [
                q_all[pl.ds(first, BLOCK_RANKS), :, pair[g]].reshape(rows, HEAD_DIMENSION)
                for g in range(2)
            ]
            both = jnp.concatenate(query, axis=0)
            panel_peak, panel_num, panel_den = block_stats(
                both, panel[0, :, at], panel[1, :, at], None
            )
            panel_peak = jnp.where(matched, panel_peak, NEG)
            own_query = jnp.concatenate(
                [jnp.dot(pick, part, preferred_element_type=F32) for part in query], axis=0
            ).astype(BF16)
            slot_valid = mask[0:slots]
            slot_valid = jnp.concatenate([slot_valid] * (2 * DECODE_STEPS), axis=0) > 0.5
            tokens = suffix.shape[1] * suffix.shape[2]
            own_peak, own_num, own_den = block_stats(
                own_query,
                suffix[0, :, :, at].reshape(tokens, HEAD_DIMENSION),
                suffix[1, :, :, at].reshape(tokens, HEAD_DIMENSION),
                slot_valid,
            )
            own_all = jnp.concatenate(
                [own_num, own_den, jnp.broadcast_to(own_peak, own_num.shape)], axis=1
            )
            own_all = jnp.concatenate(
                [
                    jnp.dot(
                        put,
                        own_all[g * rows_rank : (g + 1) * rows_rank],
                        preferred_element_type=F32,
                        precision=lax.Precision.HIGHEST,
                    )
                    for g in range(2)
                ],
                axis=0,
            )
            own_num = own_all[:, :HEAD_DIMENSION]
            own_den = own_all[:, HEAD_DIMENSION : 2 * HEAD_DIMENSION]
            own_peak = jnp.where(is_here, own_all[:, 2 * HEAD_DIMENSION :], NEG)
            fresh_peak, fresh_num, fresh_den = block_stats(
                both, fresh[0, :, at], fresh[1, :, at], fresh_valid
            )
            peak = jnp.maximum(jnp.maximum(panel_peak, fresh_peak), own_peak)
            panel_factor = jnp.where(matched, jnp.exp2((panel_peak - peak) * EXP2_SCALE), 0.0)
            own_factor = jnp.exp2((own_peak - peak) * EXP2_SCALE)
            fresh_factor = jnp.exp2((fresh_peak - peak) * EXP2_SCALE)
            num = panel_num * panel_factor + own_num * own_factor + fresh_num * fresh_factor
            den = panel_den * panel_factor + own_den * own_factor + fresh_den * fresh_factor
            lane = iota((rows, HEAD_DIMENSION), 1)
            held = stat_out[pl.ds(first, BLOCK_RANKS)].reshape(rows, HEAD_DIMENSION)
            for g in range(2):
                part = slice(g * rows, (g + 1) * rows)
                held = jnp.where(lane == 2 * h + g, peak[part], held)
                held = jnp.where(lane == 64 + 2 * h + g, den[part], held)
                num_out[pl.ds(first, BLOCK_RANKS), :, pair[g]] = (
                    num[part].astype(BF16).reshape(BLOCK_RANKS, rows_rank, HEAD_DIMENSION)
                )
            stat_out[pl.ds(first, BLOCK_RANKS)] = held.reshape(
                BLOCK_RANKS, rows_rank, HEAD_DIMENSION
            )
            return carry

        lax.fori_loop(0, kv_local, head, 0)

    stat_out[...] = jnp.zeros(stat_out.shape, F32)
    local[0].wait()
    for index, target, source in near:
        query_copy(index, target, source).wait_recv()
    for copy in local[2:5]:
        copy.wait()
    for block in range(half // BLOCK_RANKS):
        work(near_base + block * BLOCK_RANKS)
    for index, target, _ in near:
        stat_copy(index, target, me).start()
        num_copy(index, target, me).start()
    for index, target, source in far:
        query_copy(index, target, source).wait_recv()
    for block in range(half // BLOCK_RANKS):
        work(far_base + block * BLOCK_RANKS)
    for index, target, _ in far:
        stat_copy(index, target, me).start()
        num_copy(index, target, me).start()
    num_in[me] = num_out[me]
    stat_in[me] = stat_out[me]
    for index, target, source in near + far:
        stat_copy(index, target, source).wait_recv()
        num_copy(index, target, source).wait_recv()

    peak = stat_in[0]
    for rank in range(1, n_req):
        peak = jnp.maximum(peak, stat_in[rank])
    factors = [jnp.exp2((stat_in[rank] - peak) * EXP2_SCALE) for rank in range(n_req)]
    total = jnp.zeros(peak.shape, F32)
    for rank in range(n_req):
        total = total + factors[rank] * pltpu.roll(stat_in[rank], 64, 1)
    head_lanes = iota(peak.shape, 1) < 2 * kv_local
    total = jnp.where(head_lanes, total, 1.0)
    factors = [jnp.where(head_lanes, factor, 0.0) / total for factor in factors]
    for h in range(2 * kv_local):
        at = slice(h * HEAD_DIMENSION, (h + 1) * HEAD_DIMENSION)
        summed = jnp.zeros((rows_rank, HEAD_DIMENSION), F32)
        for rank in range(n_req):
            summed = summed + factors[rank][:, h : h + 1] * num_in[rank, :, at].astype(F32)
        attended[:, at] = summed.astype(BF16)

    local[6].wait()
    width = out_ref.shape[1]

    def project(target):
        columns = pl.ds(pl.multiple_of(target * width, HEAD_DIMENSION), width)
        return jnp.dot(attended[...], weight[:, columns], preferred_element_type=F32)

    for index, target, _ in mp_peers:
        part_out[target] = project(target).astype(BF16)
        part_copy(index, target, mp).start()
    result = project(mp)
    for index, target, source in mp_peers:
        part_copy(index, target, source).wait_recv()
        result = result + part_in[source].astype(F32)
    out_ref[...] = result.astype(BF16)

    for index, target, source in near + far:
        info_copy(index, target, source).wait_send()
        query_copy(index, target, source).wait_send()
        stat_copy(index, target, source).wait_send()
        num_copy(index, target, source).wait_send()
    for index, target, source in mp_peers:
        part_copy(index, target, source).wait_send()


def shards(
    queries,
    fresh_key_value,
    suffix_key_value,
    suffix_len,
    prefix_ids,
    panel_owner,
    prefix_key_value,
    out_weight,
    swap_flags,
):
    n_req = lax.axis_size("req")
    n_mp = lax.axis_size("mp")
    me = lax.axis_index("req")
    slots = queries.shape[1]
    rows_rank = DECODE_STEPS * slots
    model_lanes = queries.shape[2]
    kv_lanes = suffix_key_value.shape[3]
    width = out_weight.shape[1] // n_mp
    lanes = max(128, n_req * slots)
    info = jnp.concatenate(
        [swap_flags, prefix_ids[None], jnp.zeros((8 - DECODE_STEPS - 1, slots), jnp.int32)]
    ).astype(F32)
    info = jnp.tile(info, (1, lanes // slots))
    info = jnp.where(jnp.arange(lanes)[None] // slots == me, info, 0.0)
    slot = jnp.arange(slots * SUFFIX_SLOTS)[None]
    owner = jnp.arange(slots)[:, None]
    live = (slot // SUFFIX_SLOTS == owner) & (slot % SUFFIX_SLOTS < suffix_len[:, None])
    prefix = jnp.broadcast_to((panel_owner[0] // 2).astype(F32), live.shape)
    mask = jnp.concatenate([live.astype(F32), prefix])
    anywhere = pl.BlockSpec(memory_space=pl.ANY)
    out = pl.pallas_call(
        functools.partial(kernel, n_req, n_mp),
        out_shape=jax.ShapeDtypeStruct((rows_rank, width), BF16),
        in_specs=[anywhere] * 7,
        out_specs=pl.BlockSpec(memory_space=pltpu.VMEM),
        scratch_shapes=[
            pltpu.VMEM((n_req, rows_rank, model_lanes), BF16),
            pltpu.VMEM((n_req, 8, lanes), F32),
            pltpu.VMEM((2, PANEL_TOKENS, kv_lanes), BF16),
            pltpu.VMEM((2, slots, SUFFIX_SLOTS, kv_lanes), BF16),
            pltpu.VMEM((2, rows_rank, kv_lanes), BF16),
            pltpu.VMEM(mask.shape, F32),
            pltpu.VMEM(out_weight.shape, BF16),
            pltpu.VMEM((n_req, rows_rank, model_lanes), BF16),
            pltpu.VMEM((n_req, rows_rank, HEAD_DIMENSION), F32),
            pltpu.VMEM((n_req, rows_rank, model_lanes), BF16),
            pltpu.VMEM((n_req, rows_rank, HEAD_DIMENSION), F32),
            pltpu.VMEM((rows_rank, model_lanes), BF16),
            pltpu.VMEM((n_mp, rows_rank, width), BF16),
            pltpu.VMEM((n_mp, rows_rank, width), BF16),
            pltpu.SemaphoreType.DMA((7,)),
        ]
        + [pltpu.SemaphoreType.DMA((n_req,))] * 8
        + [pltpu.SemaphoreType.DMA((n_mp,))] * 2,
        compiler_params=pltpu.CompilerParams(
            collective_id=0, has_side_effects=True, vmem_limit_bytes=56 * 2**20
        ),
        name="cascade",
    )(
        queries.reshape(rows_rank, model_lanes),
        fresh_key_value.transpose(1, 0, 2, 3).reshape(2, rows_rank, kv_lanes),
        suffix_key_value,
        mask,
        info,
        prefix_key_value.reshape(2, PANEL_TOKENS, kv_lanes),
        out_weight,
    )
    return out.reshape(DECODE_STEPS, slots, width)


def solution(mesh):
    placed = (
        P(None, "req", "mp"),
        P(None, None, "req", "mp"),
        P(None, "req", None, "mp"),
        P("req"),
        P("req"),
        P("req"),
        P(None, "req", None, "mp"),
        P("mp", None),
        P(None, "req"),
    )
    return jax.shard_map(
        shards, mesh=mesh, in_specs=placed, out_specs=P(None, "req", "mp"), check_vma=False
    )
```

time: 568 us -> 56.1 us (0.10)
  blocking collectives: 244 us -> 0 us
  waiting for transfers between devices: 169 us -> 0 us
  local copies, waits for them, and re-layouts: 53.7 us -> 2.97 us
  Pallas kernels: 0 us -> 50.1 us
  starting transfers between devices: 31.6 us -> 0 us
  matrix products: 30.5 us -> 0 us
  other arithmetic: 22.2 us -> 2.1 us
  between operations: 16 us -> 0.73 us
    all_gather x4 -> x0, blocking collectives: 161 us -> none  [shards(): all_queries = lax.all_gather(query_matrix, 'req', axis=0, tiled=True)]
    ppermute x16 -> x0, waiting for transfers between devices: 92.7 us -> none  [partner(): return lax.ppermute(value, axis, pairs)]
    pallas_call x0 -> x1, Pallas kernels: none -> 50.1 us  [shards(): pl.pallas_call(functools.partial(kernel, n_req, n_mp), out_shape=jax.Shap...]
    unnamed x3 -> x0, waiting for transfers between devices: 48.2 us -> none
    unnamed x2 -> x0, blocking collectives: 46.4 us -> none
    pmax x1 -> x0, blocking collectives: 35.8 us -> none  [shards(): global_peak = lax.pmax(panel_peak, 'req')]
    ppermute x16 -> x0, starting transfers between devices: 31.3 us -> none  [partner(): return lax.ppermute(value, axis, pairs)]
    dot_general x17 -> x0, matrix products: 30.5 us -> none  [the longest x4 9.23 us: shards(): jnp.einsum('rkgd,tkd->rkgt', all_block, shared_panel_keys, preferred_elem...]
  transfers between devices with their start and end apart: 18 -> 0, of which waited for: 12 -> 0; matrix products, arithmetic and copies ran while one was open for 15% -> 0% of each run, Pallas kernels for 0% -> 0%
where the time goes in v1:
time: 56.1 us; the launch traced here: 55.9 us
  Pallas kernels  50.1 us (89%)
  local copies, waits for them, and re-layouts  2.97 us (5%)
  other arithmetic  2.1 us (4%)
  between operations  0.73 us (1%)
    pallas_call x1, Pallas kernels, shards(): pl.pallas_call(functools.partial(kernel, n_req, n_mp), out_shape=jax.Shap...  50.1 us
    unnamed x3, local copies, waits for them, and re-layouts  1.53 us

profile of v1, /device:TPU:0, one launch (start us, length us, event | category | flops | bytes accessed | tf_op | source)
XLA Modules:
  0.0 55.9 jit_solution(14637538136518176908)
XLA Ops:
  0.0 0.0 copy-start
  0.7 0.1 pad.3.clone
  0.8 0.8 %add_convert_fusion = f32[8,8]{1,0:T(8,128)S(1)} fusion(s32[1,8]{1,0:T(1,128)} %bitcast.17, s32[4,8]{1,0:T(4,128)} %param.17, s32[8]{0:T(128)S(1)} %pad.3.clone), kind=kLoop, calls=%fused_computation.15 | loop fusion | flops 192 | bytes 448 | tf_op jit(solution)/shard_map/convert_element_type | solution.py:399
  1.6 0.7 %fusion.1 = f32[8,1024]{1,0:T(8,128)S(1)} fusion(s32[1024]{0:T(1024)S(1)} %get-tuple-element.5, s32[1024]{0:T(1024)S(1)} %get-tuple-element.6, s32[8]{0:T(128)} %param.12), kind=kLoop, calls=%fused_computation.3 | loop fusion | flops 32768 | bytes 40992 | tf_op jit(solution)/shard_map/convert_element_type | solution.py:406
  2.3 0.6 %concatenate.14.mask_hbm = f32[16,1024]{1,0:T(8,128)} pad(f32[8,1024]{1,0:T(8,128)S(1)} %fusion.1, f32[]{:T(128)S(6)} %convert_element_type.14), padding=0_8x0_0 | pad | bytes 98308 | tf_op jit(solution)/shard_map/concatenate | solution.py:406
  2.9 0.1 tile.10
  3.0 0.6 %broadcast_select_fusion.info_hbm = f32[8,128]{1,0:T(8,128)} fusion(f32[8,128]{1,0:T(8,128)S(1)} %tile.10, pred[128]{0:T(512)(128)(4,1)S(1)} %fusion.9), kind=kLoop, calls=%fused_computation.16 | loop fusion | flops 1024 | bytes 8320 | tf_op jit(solution)/shard_map/jit(_where)/select_n | solution.py:401
  3.6 0.0 copy-done
  3.6 0.6 %copy_bitcast_fusion.fresh_hbm = bf16[2,32,512]{2,1,0:T(8,128)(2,1)} fusion(bf16[4,2,8,512]{3,2,1,0:T(8,128)(2,1)S(1)} %copy-done), kind=kLoop, calls=%fused_computation | loop fusion | bytes 131072 | tf_op jit(solution)/shard_map/reshape | solution.py:438
  4.3 50.1 %cascade.1 = bf16[32,1152]{1,0:T(8,128)(2,1)} custom-call(bf16[32,1024]{1,0:T(8,128)(2,1)} %bitcast.16, bf16[2,32,512]{2,1,0:T(8,128)(2,1)} %copy_bitcast_fusion.fresh_hbm, bf16[2,8,128,512]{3,2,1,0:T(8,128)(2,1)} %suffix_hbm.1, f32[16,1024]{1,0:T(8,128)} %concatenate.14.mask_hbm, f32[8,128]{1,0:T(8,128)} %broadcast_select_fusion.info_hbm, ...), custom_call_target="tpu_custom_call" | custom-call | tf_op jit(solution)/shard_map/cascade/pallas_call | solution.py:408
  54.3 1.5 %copy.15 = bf16[4,8,1152]{2,1,0:T(8,128)(2,1)} copy(bf16[4,8,1152]{2,1,0:T(8,128)(2,1)} %bitcast.15) | data formatting | bytes 147456
  (4 shorter events, 0.0 us)
Async XLA Ops:
  0.0 3.6 %copy-start = (bf16[4,2,8,512]{3,2,1,0:T(8,128)(2,1)S(1)}, bf16[4,2,8,512]{3,2,1,0:T(8,128)(2,1)}, u32[]{:S(2)}) copy-start(bf16[4,2,8,512]{3,2,1,0:T(8,128)(2,1)} %param.10) | copy-start | bytes 196612

commit v2 on v1

v2 whole, which is shorter than its diff:
```python
import functools
import math

import jax
import jax.numpy as jnp
from jax import lax
from jax.experimental import pallas as pl
from jax.experimental.pallas import tpu as pltpu
from jax.sharding import PartitionSpec as P

D = 4608
QUERY_HEADS = 32
HEAD_DIMENSION = 128
SUFFIX_SLOTS = 128
PANEL_TOKENS = 2048
DECODE_STEPS = 4
BLOCK_RANKS = 4

NEG = -(2.0**100)
EXP2_SCALE = (D // QUERY_HEADS) ** (-0.5) * math.log2(math.e)
MESH = pl.DeviceIdType.MESH
F32 = jnp.float32
BF16 = jnp.bfloat16


def dot_t(left, right):
    return lax.dot_general(left, right, (((1,), (1,)), ((), ())), preferred_element_type=F32)


def iota(shape, dimension):
    return lax.broadcasted_iota(jnp.int32, shape, dimension)


def block_stats(queries, keys, values, is_valid):
    scores = dot_t(queries, keys)
    if is_valid is not None:
        scores = jnp.where(is_valid, scores, NEG)
    peak = jnp.max(scores, axis=1, keepdims=True)
    weights = jnp.exp2((scores - peak) * EXP2_SCALE)
    if is_valid is not None:
        weights = jnp.where(is_valid, weights, 0.0)
    widened = jnp.concatenate([values, jnp.ones(values.shape, BF16)], axis=1)
    summed = jnp.dot(weights.astype(BF16), widened, preferred_element_type=F32)
    return peak, summed[:, :HEAD_DIMENSION], summed[:, HEAD_DIMENSION:]


def split(value):
    high = value.astype(BF16).astype(F32)
    low = (value - high).astype(BF16).astype(F32)
    return high, low, high + low


def pack(peaks, nums, dens):
    lane = iota((nums[0].shape[0], HEAD_DIMENSION), 1)
    stats = jnp.zeros(nums[0].shape, F32)
    for g in range(2):
        parts = (*split(peaks[g])[:2], *split(dens[g])[:2])
        for place, part in zip((2 * g, 2 * g + 1, 4 + 2 * g, 5 + 2 * g), parts):
            stats = jnp.where(lane == place, part, stats)
    return jnp.concatenate([nums[0], nums[1], stats], axis=1).astype(BF16)


def merge(messages):
    peaks, nums, dens = [], [], []
    stats = [message[:, 2 * HEAD_DIMENSION :].astype(F32) for message in messages]
    for g in range(2):
        tops = [stat[:, 2 * g : 2 * g + 1] + stat[:, 2 * g + 1 : 2 * g + 2] for stat in stats]
        peak = functools.reduce(jnp.maximum, tops)
        peak = split(peak)[2]
        num, den = 0.0, 0.0
        for message, stat, top in zip(messages, stats, tops):
            factor = jnp.exp2((top - peak) * EXP2_SCALE)
            den = den + factor * (stat[:, 4 + 2 * g : 5 + 2 * g] + stat[:, 5 + 2 * g : 6 + 2 * g])
            num = num + factor * message[
                :, g * HEAD_DIMENSION : (g + 1) * HEAD_DIMENSION
            ].astype(F32)
        peaks.append(peak)
        nums.append(num)
        dens.append(den)
    return peaks, nums, dens


def kernel(
    n_req,
    n_mp,
    q_hbm,
    fresh_hbm,
    suffix_hbm,
    length_hbm,
    prefix_hbm,
    owner_hbm,
    flag_hbm,
    panel_hbm,
    weight_hbm,
    out_ref,
    q_all,
    info_all,
    panel,
    suffix,
    fresh,
    length,
    prefix,
    owner,
    flag,
    weight,
    message_out,
    near_in,
    relay_in,
    final_out,
    final_in,
    attended,
    product,
    part_out,
    part_in,
    local_sem,
    q_send,
    q_recv,
    info_send,
    info_recv,
    forward_send,
    forward_recv,
    near_send,
    near_recv,
    relay_send,
    relay_recv,
    final_send,
    final_recv,
    part_send,
    part_recv,
):
    me = lax.axis_index("req")
    mp = lax.axis_index("mp")
    half = n_req // 2
    side = me // half
    place = me % half
    near_base = side * half
    far_base = (1 - side) * half
    counterpart = far_base + place
    kv_local = panel.shape[2] // HEAD_DIMENSION
    rows_rank = q_all.shape[1]
    slots = rows_rank // DECODE_STEPS
    rows = BLOCK_RANKS * rows_rank
    lanes = info_all.shape[2]

    local = [
        pltpu.make_async_copy(source, destination, local_sem.at[index])
        for index, (source, destination) in enumerate(
            [
                (flag_hbm, flag),
                (prefix_hbm, prefix),
                (length_hbm, length),
                (owner_hbm, owner),
                (q_hbm, q_all.at[me]),
                (panel_hbm, panel),
                (suffix_hbm, suffix),
                (fresh_hbm, fresh),
                (weight_hbm, weight),
            ]
        )
    ]
    for copy in local:
        copy.start()

    near = [(d, (place + d) % half, (place + half - d) % half) for d in range(1, half)]
    everyone = [
        (side_index * half + d, base + (place + d) % half, base + (place + half - d) % half)
        for side_index, base in ((1, far_base), (0, near_base))
        for d in range(1 - side_index, half)
    ]
    mp_peers = [(d, (mp + d) % n_mp, (mp + n_mp - d) % n_mp) for d in range(1, n_mp)]
    mp_peers = sorted(mp_peers, key=lambda peer: abs(peer[0] - n_mp // 2))

    barrier = pltpu.get_barrier_semaphore()
    for _, target, _ in everyone:
        pl.semaphore_signal(barrier, inc=1, device_id=(target, mp), device_id_type=MESH)
    for _, target, _ in mp_peers:
        pl.semaphore_signal(barrier, inc=1, device_id=(me, target), device_id_type=MESH)

    for copy in local[:4]:
        copy.wait()
    known = jnp.concatenate(
        [
            flag[...].astype(F32),
            prefix[...].astype(F32),
            jnp.zeros((8 - DECODE_STEPS - 1, slots), F32),
        ],
        axis=0,
    )
    lane = iota((8, lanes), 1)
    mine = jnp.zeros((8, lanes), F32)
    for k in range(slots):
        mine = jnp.where(lane == me * slots + k, known[:, k : k + 1], mine)
    info_all[me] = mine
    my_prefix = (owner[...] // 2).astype(F32)

    pl.semaphore_wait(barrier, n_req - 1 + n_mp - 1)

    def remote(source, destination, send, receive, device):
        return pltpu.make_async_remote_copy(
            src_ref=source,
            dst_ref=destination,
            send_sem=send,
            recv_sem=receive,
            device_id=device,
            device_id_type=MESH,
        )

    def info_copy(index, target, slot):
        return remote(
            info_all.at[me],
            info_all.at[slot],
            info_send.at[index],
            info_recv.at[index],
            (target, mp),
        )

    def query_copy(index, target, slot):
        return remote(
            q_hbm, q_all.at[slot], q_send.at[index], q_recv.at[index], (target, mp)
        )

    def forward_copy(index, target, slot):
        return remote(
            q_all.at[counterpart],
            q_all.at[slot],
            forward_send.at[index],
            forward_recv.at[index],
            (near_base + target, mp),
        )

    def near_copy(h, index, target, slot):
        return remote(
            message_out.at[h, near_base + target],
            near_in.at[h, slot],
            near_send.at[h, index],
            near_recv.at[h, index],
            (near_base + target, mp),
        )

    def relay_copy(h, index, target, slot):
        return remote(
            message_out.at[h, far_base + target],
            relay_in.at[h, slot],
            relay_send.at[h, index],
            relay_recv.at[h, index],
            (near_base + target, mp),
        )

    def final_copy(h):
        return remote(
            final_out.at[h], final_in.at[h], final_send.at[h], final_recv.at[h], (counterpart, mp)
        )

    def part_copy(index, target, slot):
        return remote(
            part_out.at[target],
            part_in.at[slot],
            part_send.at[index],
            part_recv.at[index],
            (me, target),
        )

    for index, target, _ in everyone:
        info_copy(index, target, me).start()
    query_copy(0, counterpart, me).start()
    for index, target, _ in near:
        query_copy(index, near_base + target, me).start()

    tokens = suffix.shape[1] * suffix.shape[2]
    column = jnp.where(
        iota((slots, slots), 0) == iota((slots, slots), 1),
        jnp.broadcast_to(length[...].astype(F32), (slots, slots)),
        0.0,
    )
    column = jnp.sum(column, axis=1, keepdims=True).astype(jnp.int32)
    slot = iota((slots, tokens), 1)
    live = (slot // SUFFIX_SLOTS == iota((slots, tokens), 0)) & (slot % SUFFIX_SLOTS < column)
    live = jnp.where(live, 1.0, 0.0)
    live = jnp.concatenate([live] * (2 * DECODE_STEPS), axis=0) > 0.5

    for index, target, source in everyone:
        info_copy(index, target, source).wait_recv()
    info = info_all[0]
    for rank in range(1, n_req):
        info = info + info_all[rank]
    state_row = iota((8, lanes), 0)
    position = iota((8, lanes), 1)
    state = jnp.where(
        state_row == 0,
        position.astype(F32),
        jnp.where(state_row == 1, jnp.broadcast_to(info[4:5], (8, lanes)), 0.0),
    )
    bit_count = n_req.bit_length() - 1
    requests = jnp.zeros((8, lanes), F32)
    for step in range(DECODE_STEPS):
        distance = slots << (step % bit_count)
        lane = iota((lanes, lanes), 1)
        partner = jnp.where((lane // distance) % 2 == 1, lane - distance, lane + distance)
        flagged = jnp.broadcast_to(info[step : step + 1], (lanes, lanes)) > 0.5
        origin = jnp.where(flagged, partner, lane)
        moves = jnp.where(iota((lanes, lanes), 0) == origin, 1.0, 0.0).astype(BF16)
        state = jnp.dot(state.astype(BF16), moves, preferred_element_type=F32)
        requests = jnp.where(state_row == step, state[0:1], requests)
        requests = jnp.where(state_row == DECODE_STEPS + step, state[1:2], requests)
    requests = requests.astype(BF16)
    token = iota((rows_rank, lanes), 0)
    token_at = jnp.where(iota((rows_rank, lanes), 1) == me * slots + token % slots, 1.0, 0.0)
    token_steps = dot_t(requests, token_at.astype(BF16))
    token_step = iota((1, rows_rank), 1) // slots
    token_request = jnp.zeros((1, rows_rank), F32)
    for step in range(DECODE_STEPS):
        token_request = jnp.where(token_step == step, token_steps[step : step + 1], token_request)

    def prepare(first):
        row = iota((rows, lanes), 0)
        row_position = (first + row // rows_rank) * slots + row % slots
        row_at = jnp.where(iota((rows, lanes), 1) == row_position, 1.0, 0.0).astype(BF16)
        down = dot_t(row_at, requests)
        across = dot_t(requests, row_at)
        down_step = (iota((rows, 1), 0) // slots) % DECODE_STEPS
        across_step = (iota((1, rows), 1) // slots) % DECODE_STEPS
        down_request = jnp.zeros((rows, 1), F32)
        down_prefix = jnp.zeros((rows, 1), F32)
        across_request = jnp.zeros((1, rows), F32)
        for step in range(DECODE_STEPS):
            here = down_step == step
            down_request = jnp.where(here, down[:, step : step + 1], down_request)
            down_prefix = jnp.where(
                here, down[:, DECODE_STEPS + step : DECODE_STEPS + step + 1], down_prefix
            )
            across_request = jnp.where(across_step == step, across[step : step + 1], across_request)
        matched = jnp.where(down_prefix == my_prefix, 1.0, 0.0)
        matched = jnp.concatenate([matched, matched], axis=0) > 0.5
        own = iota((rows_rank, rows), 0)
        pick = jnp.where(
            (across_request == (me * slots + own % slots).astype(F32))
            & (across_step == own // slots),
            1.0,
            0.0,
        ).astype(BF16)
        own = iota((rows, rows_rank), 1)
        put = jnp.where(
            (down_request == (me * slots + own % slots).astype(F32)) & (down_step == own // slots),
            1.0,
            0.0,
        )
        is_here = jnp.sum(put, axis=1, keepdims=True)
        is_here = jnp.concatenate([is_here, is_here], axis=0) > 0.5
        fresh_valid = jnp.where(
            (down_request == token_request) & (down_step >= token_step), 1.0, 0.0
        )
        fresh_valid = jnp.concatenate([fresh_valid, fresh_valid], axis=0) > 0.5
        return first, matched, pick, put, is_here, fresh_valid

    def head(h, prepared):
        first, matched, pick, put, is_here, fresh_valid = prepared
        at = slice(h * HEAD_DIMENSION, (h + 1) * HEAD_DIMENSION)
        query = [
            q_all[
                pl.ds(first, BLOCK_RANKS),
                :,
                (2 * h + g) * HEAD_DIMENSION : (2 * h + g + 1) * HEAD_DIMENSION,
            ].reshape(rows, HEAD_DIMENSION)
            for g in range(2)
        ]
        both = jnp.concatenate(query, axis=0)
        panel_peak, panel_num, panel_den = block_stats(
            both, panel[0, :, at], panel[1, :, at], None
        )
        panel_peak = jnp.where(matched, panel_peak, NEG)
        own_query = jnp.concatenate(
            [jnp.dot(pick, part, preferred_element_type=F32) for part in query], axis=0
        ).astype(BF16)
        own_peak, own_num, own_den = block_stats(
            own_query,
            suffix[0, :, :, at].reshape(tokens, HEAD_DIMENSION),
            suffix[1, :, :, at].reshape(tokens, HEAD_DIMENSION),
            live,
        )
        own_all = jnp.concatenate(
            [own_num, own_den, jnp.broadcast_to(own_peak, own_num.shape)], axis=1
        )
        own_all = jnp.concatenate(
            [
                jnp.dot(
                    put,
                    own_all[g * rows_rank : (g + 1) * rows_rank],
                    preferred_element_type=F32,
                    precision=lax.Precision.HIGHEST,
                )
                for g in range(2)
            ],
            axis=0,
        )
        own_num = own_all[:, :HEAD_DIMENSION]
        own_den = own_all[:, HEAD_DIMENSION : 2 * HEAD_DIMENSION]
        own_peak = jnp.where(is_here, own_all[:, 2 * HEAD_DIMENSION :], NEG)
        fresh_peak, fresh_num, fresh_den = block_stats(
            both, fresh[0, :, at], fresh[1, :, at], fresh_valid
        )
        peak = jnp.maximum(jnp.maximum(panel_peak, fresh_peak), own_peak)
        peak = split(peak)[2]
        panel_factor = jnp.where(matched, jnp.exp2((panel_peak - peak) * EXP2_SCALE), 0.0)
        own_factor = jnp.exp2((own_peak - peak) * EXP2_SCALE)
        fresh_factor = jnp.exp2((fresh_peak - peak) * EXP2_SCALE)
        num = panel_num * panel_factor + own_num * own_factor + fresh_num * fresh_factor
        den = panel_den * panel_factor + own_den * own_factor + fresh_den * fresh_factor
        message = pack(
            [peak[:rows], peak[rows:]], [num[:rows], num[rows:]], [den[:rows], den[rows:]]
        )
        message_out[h, pl.ds(first, BLOCK_RANKS)] = message.reshape(
            BLOCK_RANKS, rows_rank, 3 * HEAD_DIMENSION
        )

    def near_head(h):
        for prepared in near_rows:
            head(h, prepared)
        for index, target, _ in near:
            near_copy(h, index, target, place).start()

    def far_head(h):
        for prepared in far_rows:
            head(h, prepared)
        for index, target, _ in near:
            relay_copy(h, index, target, place).start()

    def relay(h):
        for index, target, source in near:
            relay_copy(h, index, target, source).wait_recv()
        messages = [message_out[h, counterpart]]
        messages += [relay_in[h, source] for _, _, source in near]
        final_out[h] = pack(*merge(messages))
        final_copy(h).start()

    def attend(h):
        for index, target, source in near:
            near_copy(h, index, target, source).wait_recv()
        final_copy(h).wait_recv()
        messages = [message_out[h, me], final_in[h]]
        messages += [near_in[h, source] for _, _, source in near]
        _, nums, dens = merge(messages)
        for g in range(2):
            at = slice((2 * h + g) * HEAD_DIMENSION, (2 * h + g + 1) * HEAD_DIMENSION)
            attended[:, at] = (nums[g] / dens[g]).astype(BF16)

    blocks = range(half // BLOCK_RANKS)
    near_rows = [prepare(near_base + block * BLOCK_RANKS) for block in blocks]
    query_copy(0, counterpart, counterpart).wait_recv()
    for index, target, _ in near:
        forward_copy(index, target, counterpart).start()
    for copy in local[4:8]:
        copy.wait()
    for index, target, source in near:
        query_copy(index, near_base + target, near_base + source).wait_recv()
    early = kv_local // 2
    for h in range(early):
        near_head(h)
    far_rows = [prepare(far_base + block * BLOCK_RANKS) for block in blocks]
    for index, target, source in near:
        forward_copy(index, target, far_base + source).wait_recv()
    for h in range(kv_local):
        far_head(h)
        if h:
            relay(h - 1)
    for h in range(early, kv_local):
        near_head(h)
        if h == early:
            relay(kv_local - 1)
    for h in range(kv_local - 1):
        attend(h)

    local[8].wait()
    width = out_ref.shape[1]
    known_lanes = (kv_local - 1) * 2 * HEAD_DIMENSION

    def project(target, rows_from, rows_to):
        columns = pl.ds(pl.multiple_of(target * width, HEAD_DIMENSION), width)
        return jnp.dot(
            attended[:, rows_from:rows_to],
            weight[rows_from:rows_to, columns],
            preferred_element_type=F32,
        )

    targets = [target for _, target, _ in mp_peers] + [mp]
    for order, target in enumerate(targets):
        product[order] = project(target, 0, known_lanes)
    attend(kv_local - 1)
    for order, (index, target, _) in enumerate(mp_peers):
        total = product[order] + project(target, known_lanes, attended.shape[1])
        part_out[target] = total.astype(BF16)
        part_copy(index, target, mp).start()
    result = product[n_mp - 1] + project(mp, known_lanes, attended.shape[1])
    for index, target, source in mp_peers:
        part_copy(index, target, source).wait_recv()
        result = result + part_in[source].astype(F32)
    out_ref[...] = result.astype(BF16)

    for index, target, source in everyone:
        info_copy(index, target, source).wait_send()
    query_copy(0, counterpart, counterpart).wait_send()
    for index, target, source in near:
        query_copy(index, near_base + target, near_base + source).wait_send()
        forward_copy(index, target, far_base + source).wait_send()
    for h in range(kv_local):
        for index, target, source in near:
            near_copy(h, index, target, source).wait_send()
            relay_copy(h, index, target, source).wait_send()
        final_copy(h).wait_send()
    for index, target, source in mp_peers:
        part_copy(index, target, source).wait_send()


def shards(
    queries,
    fresh_key_value,
    suffix_key_value,
    suffix_len,
    prefix_ids,
    panel_owner,
    prefix_key_value,
    out_weight,
    swap_flags,
):
    n_req = lax.axis_size("req")
    n_mp = lax.axis_size("mp")
    half = n_req // 2
    slots = queries.shape[1]
    rows_rank = DECODE_STEPS * slots
    model_lanes = queries.shape[2]
    kv_lanes = suffix_key_value.shape[3]
    kv_local = kv_lanes // HEAD_DIMENSION
    width = out_weight.shape[1] // n_mp
    lanes = max(128, n_req * slots)
    message = 3 * HEAD_DIMENSION
    anywhere = pl.BlockSpec(memory_space=pl.ANY)
    dma = pltpu.SemaphoreType.DMA
    out = pl.pallas_call(
        functools.partial(kernel, n_req, n_mp),
        out_shape=jax.ShapeDtypeStruct((rows_rank, width), BF16),
        in_specs=[anywhere] * 9,
        out_specs=pl.BlockSpec(memory_space=pltpu.VMEM),
        scratch_shapes=[
            pltpu.VMEM((n_req, rows_rank, model_lanes), BF16),
            pltpu.VMEM((n_req, 8, lanes), F32),
            pltpu.VMEM((2, PANEL_TOKENS, kv_lanes), BF16),
            pltpu.VMEM((2, slots, SUFFIX_SLOTS, kv_lanes), BF16),
            pltpu.VMEM((2, rows_rank, kv_lanes), BF16),
            pltpu.VMEM((1, slots), jnp.int32),
            pltpu.VMEM((1, slots), jnp.int32),
            pltpu.VMEM((1, 1), jnp.int32),
            pltpu.VMEM((DECODE_STEPS, slots), jnp.int32),
            pltpu.VMEM(out_weight.shape, BF16),
            pltpu.VMEM((kv_local, n_req, rows_rank, message), BF16),
            pltpu.VMEM((kv_local, half, rows_rank, message), BF16),
            pltpu.VMEM((kv_local, half, rows_rank, message), BF16),
            pltpu.VMEM((kv_local, rows_rank, message), BF16),
            pltpu.VMEM((kv_local, rows_rank, message), BF16),
            pltpu.VMEM((rows_rank, model_lanes), BF16),
            pltpu.VMEM((n_mp, rows_rank, width), F32),
            pltpu.VMEM((n_mp, rows_rank, width), BF16),
            pltpu.VMEM((n_mp, rows_rank, width), BF16),
            dma((9,)),
        ]
        + [dma((half,))] * 2
        + [dma((n_req,))] * 2
        + [dma((half,))] * 2
        + [dma((kv_local, half))] * 4
        + [dma((kv_local,))] * 2
        + [dma((n_mp,))] * 2,
        compiler_params=pltpu.CompilerParams(
            collective_id=0, has_side_effects=True, vmem_limit_bytes=56 * 2**20
        ),
        name="cascade",
    )(
        queries.reshape(rows_rank, model_lanes),
        fresh_key_value.transpose(1, 0, 2, 3).reshape(2, rows_rank, kv_lanes),
        suffix_key_value,
        suffix_len.reshape(1, slots),
        prefix_ids.reshape(1, slots),
        panel_owner.reshape(1, 1),
        swap_flags,
        prefix_key_value.reshape(2, PANEL_TOKENS, kv_lanes),
        out_weight,
    )
    return out.reshape(DECODE_STEPS, slots, width)


def solution(mesh):
    placed = (
        P(None, "req", "mp"),
        P(None, None, "req", "mp"),
        P(None, "req", None, "mp"),
        P("req"),
        P("req"),
        P("req"),
        P(None, "req", None, "mp"),
        P("mp", None),
        P(None, "req"),
    )
    return jax.shard_map(
        shards, mesh=mesh, in_specs=placed, out_specs=P(None, "req", "mp"), check_vma=False
    )
```

time: 56.1 us -> 44.6 us (0.80)
  Pallas kernels: 50.1 us -> 41.2 us
  other arithmetic: 2.1 us -> 0 us
  local copies, waits for them, and re-layouts: 2.97 us -> 2.31 us
    pallas_call x1, Pallas kernels: 50.1 us -> 41.2 us  [shards(): pl.pallas_call(functools.partial(kernel, n_req, n_mp), out_shape=jax.Shap...]
    convert_element_type x2 -> x0, other arithmetic: 1.5 us -> none  [the longest x1 0.77 us: shards(): info = jnp.concatenate([swap_flags, prefix_ids[None], jnp.zeros((8 - DECO...]
    concatenate x3 -> x0, local copies, waits for them, and re-layouts: 0.71 us -> none  [the longest x1 0.63 us: shards(): mask = jnp.concatenate([live.astype(F32), prefix])]
    select_n x2 -> x0, other arithmetic: 0.6 us -> none  [the longest x1 0.6 us: shards(): info = jnp.where(jnp.arange(lanes)[None] // slots == me, info, 0.0)]
where the time goes in v2:
time: 44.6 us; the launch traced here: 44.2 us
  Pallas kernels  41.2 us (92%)
  local copies, waits for them, and re-layouts  2.31 us (5%)
  between operations  0.69 us (2%)
    pallas_call x1, Pallas kernels, shards(): pl.pallas_call(functools.partial(kernel, n_req, n_mp), out_shape=jax.Shap...  41.2 us
    unnamed x3, local copies, waits for them, and re-layouts  1.68 us

profile of v2, /device:TPU:0, one launch (start us, length us, event | category | flops | bytes accessed | tf_op | source)
XLA Modules:
  0.0 44.2 jit_solution(3822180164904802487)
XLA Ops:
  0.0 0.0 copy-start
  0.7 0.2 copy-done
  0.8 0.6 %copy_bitcast_fusion.fresh_hbm = bf16[2,32,512]{2,1,0:T(8,128)(2,1)} fusion(bf16[4,2,8,512]{3,2,1,0:T(8,128)(2,1)S(1)} %copy-done), kind=kLoop, calls=%fused_computation | loop fusion | bytes 131072 | tf_op jit(solution)/shard_map/reshape | solution.py:576
  1.5 41.2 %cascade.1 = bf16[32,1152]{1,0:T(8,128)(2,1)} custom-call(bf16[32,1024]{1,0:T(8,128)(2,1)} %bitcast.14, bf16[2,32,512]{2,1,0:T(8,128)(2,1)} %copy_bitcast_fusion.fresh_hbm, bf16[2,8,128,512]{3,2,1,0:T(8,128)(2,1)} %suffix_hbm.1, s32[1,8]{1,0:T(1,128)} %bitcast.15, s32[1,8]{1,0:T(1,128)} %bitcast.16, s32[1,1]{1,0:T(1,128)} %bitcast.11.owner_hbm, ...), custom_call_target="tpu_custom_call" | custom-call | tf_op jit(solution)/shard_map/cascade/pallas_call | solution.py:537
  42.7 1.5 %copy.14 = bf16[4,8,1152]{2,1,0:T(8,128)(2,1)} copy(bf16[4,8,1152]{2,1,0:T(8,128)(2,1)} %bitcast.13) | data formatting | bytes 147456
Async XLA Ops:
  0.0 0.8 %copy-start = (bf16[4,2,8,512]{3,2,1,0:T(8,128)(2,1)S(1)}, bf16[4,2,8,512]{3,2,1,0:T(8,128)(2,1)}, u32[]{:S(2)}) copy-start(bf16[4,2,8,512]{3,2,1,0:T(8,128)(2,1)} %param.10) | copy-start | bytes 196612

commit v3 on v2

--- a/solution.py
+++ b/solution.py
@@ -48,6 +48,13 @@
     high = value.astype(BF16).astype(F32)
     low = (value - high).astype(BF16).astype(F32)
     return high, low, high + low
+
+
+def three_parts(value):
+    high = value.astype(BF16).astype(F32)
+    rest = value - high
+    middle = rest.astype(BF16).astype(F32)
+    return jnp.concatenate([high, middle, rest - middle], axis=0).astype(BF16)
 
 
 def pack(peaks, nums, dens):
@@ -377,16 +384,16 @@
             suffix[1, :, :, at].reshape(tokens, HEAD_DIMENSION),
             live,
         )
+        put_thrice = jnp.concatenate([put, put, put], axis=1).astype(BF16)
         own_all = jnp.concatenate(
             [own_num, own_den, jnp.broadcast_to(own_peak, own_num.shape)], axis=1
         )
         own_all = jnp.concatenate(
             [
                 jnp.dot(
-                    put,
-                    own_all[g * rows_rank : (g + 1) * rows_rank],
+                    put_thrice,
+                    three_parts(own_all[g * rows_rank : (g + 1) * rows_rank]),
                     preferred_element_type=F32,
-                    precision=lax.Precision.HIGHEST,
                 )
                 for g in range(2)
             ],

time: 44.6 us -> 43.3 us (0.971)
  Pallas kernels: 41.2 us -> 40 us
    pallas_call x1, Pallas kernels: 41.2 us -> 40 us  [shards(): pl.pallas_call(functools.partial(kernel, n_req, n_mp), out_shape=jax.Shap...]
where the time goes in v3:
time: 43.3 us; the launch traced here: 43 us
  Pallas kernels  40 us (92%)
  local copies, waits for them, and re-layouts  2.31 us (5%)
  between operations  0.69 us (2%)
    pallas_call x1, Pallas kernels, shards(): pl.pallas_call(functools.partial(kernel, n_req, n_mp), out_shape=jax.Shap...  40 us
    unnamed x3, local copies, waits for them, and re-layouts  1.68 us

profile of v3, /device:TPU:0, one launch (start us, length us, event | category | flops | bytes accessed | tf_op | source)
XLA Modules:
  0.0 43.0 jit_solution(7775358394955985002)
XLA Ops:
  0.0 0.0 copy-start
  0.7 0.2 copy-done
  0.8 0.6 %copy_bitcast_fusion.fresh_hbm = bf16[2,32,512]{2,1,0:T(8,128)(2,1)} fusion(bf16[4,2,8,512]{3,2,1,0:T(8,128)(2,1)S(1)} %copy-done), kind=kLoop, calls=%fused_computation | loop fusion | bytes 131072 | tf_op jit(solution)/shard_map/reshape | solution.py:583
  1.5 40.0 %cascade.1 = bf16[32,1152]{1,0:T(8,128)(2,1)} custom-call(bf16[32,1024]{1,0:T(8,128)(2,1)} %bitcast.14, bf16[2,32,512]{2,1,0:T(8,128)(2,1)} %copy_bitcast_fusion.fresh_hbm, bf16[2,8,128,512]{3,2,1,0:T(8,128)(2,1)} %suffix_hbm.1, s32[1,8]{1,0:T(1,128)} %bitcast.15, s32[1,8]{1,0:T(1,128)} %bitcast.16, s32[1,1]{1,0:T(1,128)} %bitcast.11.owner_hbm, ...), custom_call_target="tpu_custom_call" | custom-call | tf_op jit(solution)/shard_map/cascade/pallas_call | solution.py:544
  41.5 1.5 %copy.14 = bf16[4,8,1152]{2,1,0:T(8,128)(2,1)} copy(bf16[4,8,1152]{2,1,0:T(8,128)(2,1)} %bitcast.13) | data formatting | bytes 147456
Async XLA Ops:
  0.0 0.8 %copy-start = (bf16[4,2,8,512]{3,2,1,0:T(8,128)(2,1)S(1)}, bf16[4,2,8,512]{3,2,1,0:T(8,128)(2,1)}, u32[]{:S(2)}) copy-start(bf16[4,2,8,512]{3,2,1,0:T(8,128)(2,1)} %param.10) | copy-start | bytes 196612
